TPU v7x, 256 devices: a whole 4x4x8 slice. The times are simulated.
256 devices in a mesh: ctx: 128 (over x, y, z), head: 2 (over core).
Axes of the slice: x: 4, y: 4, z: 8, core: 2. Of those that a mesh axis runs over, the one named last changes fastest.
Arguments:
- tokens: bfloat16 [65536, 2048], P('ctx', 'head'), may hold values from -6 to 6
- w_query: bfloat16 [2048, 256], P(None, 'head'), may hold values from -0.125 to 0.125
- w_key: bfloat16 [2048, 256], P(None, 'head'), may hold values from -0.125 to 0.125
- w_value: bfloat16 [2048, 2048], P(None, 'head'), may hold values from -0.125 to 0.125
- conv_query: bfloat16 [3, 256], P(None, 'head'), may hold values from -3 to 3
- conv_key: bfloat16 [3, 256], P(None, 'head'), may hold values from -3 to 3
- conv_value: bfloat16 [3, 2048], P(None, 'head'), may hold values from -3 to 3
- w_out: bfloat16 [2048, 2048], P('head'), may hold values from -1.3258252 to 1.3258252
- gain: bfloat16 [2048], P('head'), may hold values from 0.099609375 to 1.8984375
Outputs:
- mixed: bfloat16 [65536, 2048], P('ctx', 'head')
All inputs are finite; a program needn't handle non-finite values.
Results may differ from a plain program's by a relative error of at most 0.011.
Values may be sent and summed in bfloat16 or wider, within the bound.
A program may use at most 192 MiB of HBM per device.

v0:
```python
import math

import jax
import jax.numpy as jnp
import numpy as np
from jax import lax
from jax.sharding import Mesh
from jax.sharding import PartitionSpec as P

D = 2048
FD = 16
DV = 128
CTX = ("ctx_0", "ctx_1", "ctx_2")


def laid_out(parts, dim):
    shape = list(parts.shape[1:])
    shape[dim] *= parts.shape[0]
    return jnp.moveaxis(parts, 0, dim).reshape(shape)


def sent_to_all(array, axis):
    copies = jnp.broadcast_to(array, (lax.axis_size(axis), *array.shape))
    return lax.all_to_all(copies, axis, split_axis=0, concat_axis=0, tiled=True)


def gathered_copies(array, axis, dim):
    return laid_out(sent_to_all(array, axis), dim)


def shifted(block, axis, distance):
    devices = range(lax.axis_size(axis))
    route = [(i - distance, i) for i in devices if i - distance in devices]
    return lax.ppermute(block, axis, route)


def nothing_yet(array, identity):
    return jax.tree.map(
        lambda a, e: jnp.broadcast_to(jnp.asarray(e, a.dtype), a.shape), array, identity
    )


def entering(array, axes, combine, identity):
    before = start = nothing_yet(array, identity)
    subtotal = array
    for axis in reversed(axes):
        peers, position = (lax.axis_size(axis), lax.axis_index(axis))
        pieces = jax.tree.map(lambda part: lax.all_gather(part, axis), subtotal)
        inside, subtotal = (start, start)
        for k in range(peers):
            passed = k < position
            subtotal = combine(subtotal, jax.tree.map(lambda part: part[k], pieces))
            inside = jax.tree.map(lambda new, old: jnp.where(passed, new, old), subtotal, inside)
        before = combine(inside, before)
    return before


def in_blocks(array, dim, peers):
    shape = array.shape
    parts = array.reshape(*shape[:dim], peers, shape[dim] // peers, *shape[dim + 1 :])
    return jnp.moveaxis(parts, dim, 0)


def sent_and_summed(array, axis, dim):
    parts = in_blocks(array, dim, lax.axis_size(axis))
    arrived = lax.all_to_all(parts, axis, split_axis=0, concat_axis=0, tiled=True)
    return arrived.astype(jnp.float32).sum(axis=0)


def gathered_total(array, axis):
    return lax.all_gather(array, axis).sum(0)


def taylor_tables(width):
    left_list = [0]
    right_list = [0]
    scale_list = [1.0]
    for index in range(width):
        left_list.append(0)
        right_list.append(index + 1)
        scale_list.append(float(np.float32(width ** (-0.25))))
    for index in range(width):
        for other in range(index, width):
            left_list.append(index + 1)
            right_list.append(other + 1)
            if other == index:
                scale_list.append(1.0 / math.sqrt(2.0 * width))
            else:
                scale_list.append(1.0 / math.sqrt(width))
    count = len(left_list)
    left_table = np.zeros((width + 1, count), np.float32)
    right_table = np.zeros((width + 1, count), np.float32)
    left_table[np.array(left_list), np.arange(count)] = 1.0
    right_table[np.array(right_list), np.arange(count)] = 1.0
    return (left_table, right_table, np.array(scale_list, np.float32))


def taylor_features(u):
    width = u.shape[-1]
    left_table, right_table, scale_row = taylor_tables(width)
    extended = jnp.concatenate([jnp.ones(u.shape[:-1] + (1,), jnp.float32), u], -1)
    hp = lax.Precision.HIGHEST
    left_part = jnp.einsum("the,ef->thf", extended, jnp.asarray(left_table), precision=hp)
    right_part = jnp.einsum("the,ef->thf", extended, jnp.asarray(right_table), precision=hp)
    return (left_part * right_part * jnp.asarray(scale_row)).astype(jnp.bfloat16)


def causal_conv(projected, before, taps):
    padded = jnp.concatenate([before, projected], 0).astype(jnp.float32)
    tapf = taps.astype(jnp.float32)
    length = projected.shape[0]
    return (
        tapf[0] * padded[2 : 2 + length]
        + tapf[1] * padded[1 : 1 + length]
        + tapf[2] * padded[0:length]
    )


def body(tokens, w_query, w_key, w_value, conv_query, conv_key, conv_value, w_out, gain):
    hp = lax.Precision.HIGHEST
    rows = tokens.shape[0]
    qk_cols = w_query.shape[1]
    local_heads = qk_cols // FD
    piece = gathered_copies(tokens, "head", 1)
    qsum = jnp.dot(piece, w_query, preferred_element_type=jnp.float32)
    ksum = jnp.dot(piece, w_key, preferred_element_type=jnp.float32)
    vsum = jnp.dot(piece, w_value, preferred_element_type=jnp.float32)
    qp = qsum.astype(jnp.bfloat16)
    kp = ksum.astype(jnp.bfloat16)
    vp = vsum.astype(jnp.bfloat16)
    edge = jnp.concatenate([qp[rows - 2 :], kp[rows - 2 :], vp[rows - 2 :]], 1)
    before = shifted(edge, CTX, 1)
    query = causal_conv(qp, before[:, :qk_cols], conv_query).reshape(rows, local_heads, FD)
    keyed = causal_conv(kp, before[:, qk_cols : 2 * qk_cols], conv_key).reshape(
        rows, local_heads, FD
    )
    values = (
        causal_conv(vp, before[:, 2 * qk_cols :], conv_value)
        .astype(jnp.bfloat16)
        .reshape(rows, local_heads, DV)
    )
    pq = taylor_features(query)
    pk = taylor_features(keyed)
    local_state = jnp.einsum("shf,shd->hfd", pk, values, preferred_element_type=jnp.float32)
    local_norm = jnp.sum(pk.astype(jnp.float32), 0)

    def combine(earlier, later):
        return (earlier[0] + later[0], earlier[1] + later[1])

    identity = (jnp.zeros_like(local_state), jnp.zeros_like(local_norm))
    state, normer = entering((local_state, local_norm), CTX, combine, identity)
    causal = jnp.arange(rows)[:, None] >= jnp.arange(rows)[None, :]
    scores = jnp.einsum("thf,shf->hts", pq, pk, preferred_element_type=jnp.float32)
    scores = jnp.where(causal[None], scores, jnp.float32(0.0))
    pqf = pq.astype(jnp.float32)
    numer = jnp.einsum(
        "hts,shd->thd", scores.astype(jnp.bfloat16), values, preferred_element_type=jnp.float32
    )
    numer = numer + jnp.einsum("thf,hfd->thd", pqf, state, precision=hp)
    denom = jnp.sum(scores, -1).T + jnp.einsum("thf,hf->th", pqf, normer, precision=hp)
    mixed_heads = (numer / denom[:, :, None]).astype(jnp.bfloat16).reshape(rows, local_heads * DV)
    terms = jnp.dot(mixed_heads, w_out, preferred_element_type=jnp.float32)
    gainf = gain.astype(jnp.float32)
    share = sent_and_summed(terms.astype(jnp.bfloat16), "head", 1)
    squares = gathered_total(jnp.sum(share * share, -1), "head")
    scale = lax.rsqrt(squares[:, None] / D + 1e-05)
    return (share * scale * gainf).astype(jnp.bfloat16)


def solution(mesh):
    finer = Mesh(
        mesh.devices.reshape(4, 4, 8, mesh.shape["head"]), ("ctx_0", "ctx_1", "ctx_2", "head")
    )
    return jax.shard_map(
        body,
        mesh=finer,
        in_specs=(
            P(CTX, "head"),
            P(None, "head"),
            P(None, "head"),
            P(None, "head"),
            P(None, "head"),
            P(None, "head"),
            P(None, "head"),
            P("head", None),
            P("head"),
        ),
        out_specs=P(CTX, "head"),
        check_vma=False,
    )
```

profile of v0, /device:TPU:5, one launch (start us, length us, event | category | flops | bytes accessed | tf_op | source)
XLA Modules:
  0.0 232.9 jit_solution(6667007201211384633)
XLA Ops:
  6.5 1.6 copy.27
  8.1 0.1 broadcast_in_dim.18
  8.3 6.0 %all_to_all.10 = bf16[2,512,1024]{1,2,0:T(8,128)(2,1)S(1)} all-to-all(bf16[2,512,1024]{1,2,0:T(8,128)(2,1)S(1)} %broadcast_in_dim.18), channel_id=1, replica_groups=mesh['ctx_0'=4,'ctx_1'=4,'ctx_2'=8,'head'=2] {'head'}, dimensions={0} | all-to-all | bytes 4194304 | tf_op jit(solution)/shard_map/all_to_all | solution.py:24
  14.2 2.3 %convolution_convert_fusion.1 = bf16[512,1024]{1,0:T(8,128)(2,1)S(1)} fusion(bf16[512,2048]{0,1:T(8,128)(2,1)S(1)} %bitcast.86, bf16[2048,1024]{1,0:T(8,128)(2,1)S(1)} %copy-done.14), kind=kOutput, calls=%fused_computation.21 | convolution fusion | flops 2148007936 | bytes 7340032 | tf_op jit(solution)/shard_map/dot_general | solution.py:127
  16.7 0.8 convolution_convert_fusion.3
  17.4 0.2 copy-done.6
  17.6 0.8 convolution_convert_fusion.2
  18.4 3.5 %collective-permute-start = (bf16[2,1280]{1,0:T(2,128)(2,1)S(1)}, bf16[2,1280]{1,0:T(2,128)(2,1)S(1)}, u32[]{:S(2)}, u32[]{:S(2)}) collective-permute-start(bf16[2,1280]{1,0:T(2,128)(2,1)S(1)} %pad_maximum_fusion), channel_id=1, source_target_pairs={{0,2},{2,4},{4,6},{6,8},{8,10},{10,12},{12,14},{14,16},{16,18},{18... | collective-permute-start | bytes 15368 | tf_op jit(solution)/shard_map/ppermute | solution.py:34
  22.0 7.3 %collective-permute-done = bf16[2,1280]{1,0:T(2,128)(2,1)S(1)} collective-permute-done((bf16[2,1280]{1,0:T(2,128)(2,1)S(1)}, bf16[2,1280]{1,0:T(2,128)(2,1)S(1)}, u32[]{:S(2)}, u32[]{:S(2)}) %collective-permute-start) | collective-permute-done | bytes 5152 | tf_op jit(solution)/shard_map/ppermute | solution.py:34
  29.3 0.1 maximum_convert_fusion.1
  29.4 0.1 fusion.25
  29.5 0.1 copy.29
  29.7 0.3 maximum_convert_fusion
  30.0 0.2 copy-done.7
  30.2 2.6 %fusion.20 = f32[512,8,153]{0,2,1:T(8,128)S(1)} fusion(f32[17,153,1]{1,0,2:T(8,128)S(1)} %copy-done.7, f32[512,8,16]{0,2,1:T(8,128)S(1)} %bitcast.92), kind=kOutput, calls=%fused_computation.53 | convolution fusion | flops 127844352 | bytes 2779300 | tf_op jit(solution)/shard_map/the,ef->thf/dot_general | solution.py:103
  32.9 2.9 %convert_reduce_fusion.1 = (f32[8,153]{1,0:T(8,128)S(1)}, bf16[512,8,153]{0,2,1:T(8,128)(2,1)S(1)}) fusion(f32[153]{0:T(256)S(1)} %copy-done.10, f32[512,8,153]{0,2,1:T(8,128)S(1)} %fusion.20, f32[17,153,1]{1,0,2:T(8,128)S(1)} %copy-done.8, f32[512,8,16]{0,2,1:T(8,128)S(1)} %bitcast.93), kind=kOutput, calls=%fused_computation.7 | convolution fusion | flops 130976568 | bytes 4038184 | tf_op jit(solution)/shard_map/the,ef->thf/dot_general | solution.py:104
  35.8 0.7 fusion.7
  36.5 1.0 copy-done.4
  37.5 0.5 fusion.9
  38.0 1.2 copy.33
  39.3 0.0 all-gather.8.cloned.1.call-start
  39.3 64.7 %all-gather.12.cloned.1.call-done = f32[64,153,128]{2,0,1:T(8,128)} async-done(((f32[8,153,128]{2,0,1:T(8,128)}), f32[64,153,128]{2,0,1:T(8,128)}) %all-gather.12.cloned.1.call-update) | async-done | bytes 5013520 | tf_op jit(solution)/shard_map/all_gather | solution.py:48
  104.0 3.7 %fusion.17 = (f32[1,8,153,128]{3,1,2,0:T(8,128)}, f32[8,153,128]{2,0,1:T(8,128)}) fusion(f32[64,153,128]{2,0,1:T(8,128)} %all-gather.12.cloned.1.call-done), kind=kLoop, calls=%fused_computation.43 | loop fusion | flops 1096704 | bytes 6266880 | tf_op jit(solution)/shard_map/add | solution.py:148
  107.8 0.0 all-gather.10.cloned.1.call-start
  107.8 38.7 %all-gather.8.cloned.1.call-done = f32[4,8,153,128]{3,1,2,0:T(8,128)} async-done(((f32[1,8,153,128]{3,1,2,0:T(8,128)}), f32[4,8,153,128]{3,1,2,0:T(8,128)}) %all-gather.8.cloned.1.call-update) | async-done | bytes 2506768 | tf_op jit(solution)/shard_map/all_gather | solution.py:48
  146.5 2.6 %slice_add_fusion.3 = f32[1,8,153,128]{3,1,2,0:T(8,128)} fusion(f32[4,8,153,128]{3,1,2,0:T(8,128)} %all-gather.8.cloned.1.call-done), kind=kLoop, calls=%fused_computation.39 | loop fusion | flops 470016 | bytes 3133440 | tf_op jit(solution)/shard_map/add | solution.py:148
  149.2 0.1 iota_compare_fusion
  149.3 0.1 fusion.27
  149.4 0.1 copy.28
  149.5 20.4 %all-gather.1 = f32[64,153]{1,0:T(8,128)S(1)} all-gather(f32[8,153]{1,0:T(8,128)S(1)} %get-tuple-element.22), channel_id=3, replica_groups=mesh['ctx_0'=4,'ctx_1'=4,'ctx_2'=8,'head'=2] {'ctx_2'}, dimensions={0}, use_global_device_ids=true | all-gather | bytes 44064 | tf_op jit(solution)/shard_map/all_gather | solution.py:48
  169.9 9.0 %all_gather.40 = f32[4,8,153]{2,1,0:T(8,128)S(1)} all-gather(f32[1,8,153]{2,1,0:T(8,128)S(1)} %get-tuple-element.7), channel_id=1, replica_groups=mesh['ctx_0'=4,'ctx_1'=4,'ctx_2'=8,'head'=2] {'ctx_1'}, dimensions={0}, use_global_device_ids=true | all-gather | bytes 24480 | tf_op jit(solution)/shard_map/all_gather | solution.py:48
  179.0 9.6 %all_gather.41 = f32[4,8,153]{2,1,0:T(8,128)S(1)} all-gather(f32[1,8,153]{2,1,0:T(8,128)S(1)} %slice_add_fusion.16), channel_id=1, replica_groups=mesh['ctx_0'=4,'ctx_1'=4,'ctx_2'=8,'head'=2] {'ctx_0'}, dimensions={0}, use_global_device_ids=true | all-gather | bytes 24480 | tf_op jit(solution)/shard_map/all_gather | solution.py:48
  188.6 2.6 %fusion.23 = f32[512,8,153]{0,2,1:T(8,128)S(1)} fusion(f32[17,153,1]{1,0,2:T(8,128)S(1)} %copy-done.7, f32[512,8,16]{0,2,1:T(8,128)S(1)} %bitcast.90), kind=kOutput, calls=%fused_computation.56 | convolution fusion | flops 127844352 | bytes 2779300 | tf_op jit(solution)/shard_map/the,ef->thf/dot_general | solution.py:103
  191.2 2.6 %multiply_convert_fusion.1 = bf16[512,8,153]{0,2,1:T(8,128)(2,1)S(1)} fusion(f32[512,8,153]{0,2,1:T(8,128)S(1)} %fusion.23, f32[17,153,1]{1,0,2:T(8,128)S(1)} %copy-done.8, f32[153]{0:T(256)S(1)} %copy-done.10, f32[512,8,16]{0,2,1:T(8,128)S(1)} %bitcast.91), kind=kOutput, calls=%fused_computation.9 | convolution fusion | flops 129724416 | bytes 4033288 | tf_op jit(solution)/shard_map/the,ef->thf/dot_general | solution.py:104
  193.8 0.6 fusion.35
  194.4 1.5 select_reduce_fusion
  196.0 2.2 fusion
  198.1 3.8 %fusion.16 = f32[8,153,128]{2,0,1:T(8,128)S(1)} fusion(f32[4,8,153,128]{3,1,2,0:T(8,128)} %all-gather.10.cloned.1.call-done, f32[1,8,153,128]{3,1,2,0:T(8,128)} %get-tuple-element.5, f32[8,153,128]{2,0,1:T(8,128)} %get-tuple-element.6, f32[4,8,153,128]{3,1,2,0:T(8,128)S(1)} %copy-done.1, f32[64,153,128]{2,0,1:T(8,128)} %all-gather.12.cloned.1.call-done, ...), kind=kLoop, calls=%fused_computation.36 | loop fusion | flops 4543488 | bytes 10653712 | tf_op jit(solution)/shard_map/add | solution.py:148
  201.9 0.3 copy-done.16
  202.2 1.3 fusion.6
  203.5 0.9 copy-done.15
  204.4 2.4 %convolution_convert_fusion = bf16[512,2048]{1,0:T(8,128)(2,1)S(1)} fusion(bf16[512,1024]{0,1:T(8,128)(2,1)S(1)} %bitcast.99, bf16[1024,2048]{1,0:T(8,128)(2,1)S(1)} %copy-done.15), kind=kOutput, calls=%fused_computation.6 | convolution fusion | flops 2148532224 | bytes 7340032 | tf_op jit(solution)/shard_map/dot_general | solution.py:162
  206.9 0.2 copy.55
  207.1 15.5 %all_to_all.11 = bf16[2,512,1024]{2,1,0:T(8,128)(2,1)S(1)} all-to-all(bf16[2,512,1024]{2,1,0:T(8,128)(2,1)S(1)} %bitcast.89), channel_id=1, replica_groups=mesh['ctx_0'=4,'ctx_1'=4,'ctx_2'=8,'head'=2] {'head'}, dimensions={0} | all-to-all | bytes 4194304 | tf_op jit(solution)/shard_map/all_to_all | solution.py:66
  222.6 0.5 convert_reduce_fusion
  223.0 0.2 multiply_reduce_fusion
  223.2 1.8 all-gather.3
  225.1 1.2 multiply_convert_fusion.2
  (52 shorter events, 0.3 us)
Async XLA Ops:
  6.5 10.1 %copy-start = (bf16[2048,128]{1,0:T(8,128)(2,1)S(1)}, bf16[2048,128]{1,0:T(8,128)(2,1)}, u32[]{:S(2)}) copy-start(bf16[2048,128]{1,0:T(8,128)(2,1)} %param.16) | copy-start | bytes 1572868
  6.5 97.5 %all-gather.12.cloned.1.call-start = ((), (), s32[]{:S(2)}) async-start(), calls=%async_computation.4 | async-start | bytes 5640192 | tf_op jit(solution)/shard_map/all_gather | solution.py:48
  8.2 6.0 %copy-start.14 = (bf16[2048,1024]{1,0:T(8,128)(2,1)S(1)}, bf16[2048,1024]{1,0:T(8,128)(2,1)}, u32[]{:S(2)}) copy-start(bf16[2048,1024]{1,0:T(8,128)(2,1)} %param.18) | copy-start | bytes 12582916
  16.6 1.0 copy-start.6
  16.6 5.4 %copy-start.12 = (bf16[3,128]{1,0:T(4,128)(2,1)S(1)}, bf16[3,128]{1,0:T(4,128)(2,1)}, u32[]{:S(2)}) copy-start(bf16[3,128]{1,0:T(4,128)(2,1)} %param.20) | copy-start | bytes 2308
  16.6 5.4 %copy-start.9 = (bf16[3,1024]{1,0:T(4,128)(2,1)S(1)}, bf16[3,1024]{1,0:T(4,128)(2,1)}, u32[]{:S(2)}) copy-start(bf16[3,1024]{1,0:T(4,128)(2,1)} %param.21) | copy-start | bytes 18436
  18.4 10.9 %collective-permute-start = (bf16[2,1280]{1,0:T(2,128)(2,1)S(1)}, bf16[2,1280]{1,0:T(2,128)(2,1)S(1)}, u32[]{:S(2)}, u32[]{:S(2)}) collective-permute-start(bf16[2,1280]{1,0:T(2,128)(2,1)S(1)} %pad_maximum_fusion), channel_id=1, source_target_pairs={{0,2},{2,4},{4,6},{6,8},{8,10},{10,12},{12,14},{14,16},{16,18},{18... | collective-permute-start | bytes 15368 | tf_op jit(solution)/shard_map/ppermute | solution.py:34
  29.5 0.7 copy-start.7
  30.0 2.9 %copy-start.8 = (f32[17,153,1]{1,0,2:T(8,128)S(1)}, f32[17,153,1]{1,0,2:T(8,128)}, u32[]{:S(2)}) copy-start(f32[17,153,1]{1,0,2:T(8,128)} %constant.57) | copy-start | bytes 31216
  30.0 2.9 %copy-start.10 = (f32[153]{0:T(256)S(1)}, f32[153]{0:T(256)}, u32[]{:S(2)}) copy-start(f32[153]{0:T(256)} %constant.51.clone) | copy-start | bytes 1840
  36.5 1.0 copy-start.4
  39.3 107.2 %all-gather.8.cloned.1.call-start = ((), (), s32[]{:S(2)}) async-start(), calls=%async_computation.2 | async-start | bytes 3133440 | tf_op jit(solution)/shard_map/all_gather | solution.py:48
  107.7 41.4 %copy-start.13 = (bf16[3,128]{1,0:T(4,128)(2,1)S(1)}, bf16[3,128]{1,0:T(4,128)(2,1)}, u32[]{:S(2)}) copy-start(bf16[3,128]{1,0:T(4,128)(2,1)} %param.19) | copy-start | bytes 2308
  107.7 41.5 %copy-start.11 = (bf16[1024]{0:T(1024)(128)(2,1)S(1)}, bf16[1024]{0:T(1024)(128)(2,1)}, u32[]{:S(2)}) copy-start(bf16[1024]{0:T(1024)(128)(2,1)} %param.23) | copy-start | bytes 6148
  107.8 90.4 %all-gather.10.cloned.1.call-start = ((), (), s32[]{:S(2)}) async-start(), calls=%async_computation.3 | async-start | bytes 3133440 | tf_op jit(solution)/shard_map/all_gather | solution.py:48
  193.8 2.1 copy-start.2
  194.4 1.5 copy-start.5
  195.9 2.2 copy-start.1
  198.1 3.8 %copy-start.3 = (bf16[512,8,153]{0,2,1:T(8,128)(2,1)S(1)}, bf16[512,8,153]{0,2,1:T(8,128)(2,1)}, u32[]{:S(2)}) copy-start(bf16[512,8,153]{0,2,1:T(8,128)(2,1)} %copy-done.2) | copy-start | bytes 3760132
  198.1 4.1 %copy-start.16 = (f32[8,128,512]{2,1,0:T(8,128)S(1)}, f32[8,128,512]{2,1,0:T(8,128)}, u32[]{:S(2)}) copy-start(f32[8,128,512]{2,1,0:T(8,128)} %fusion) | copy-start | bytes 6291460
  202.2 2.2 copy-start.15
Sparse Core Ops, SparseCore 0:
  39.4 64.5 all-gather.11
  107.9 38.5 all-gather.7
  149.2 35.7 all-gather.9
where the time goes:
time: 236 us; the launch traced here: 233 us
  waiting for transfers between devices  111 us (47%)
  blocking collectives  62.3 us (26%)
  matrix products  23.1 us (10%)
  between operations  13.6 us (6%)
  other arithmetic  13.3 us (6%)
  local copies, waits for them, and re-layouts  6.14 us (3%)
  starting transfers between devices  3.64 us (2%)
    all_gather x3, waiting for transfers between devices, entering(): pieces = jax.tree.map(lambda part: lax.all_gather(part, axis), subtotal)  103 us
    all_gather x3, blocking collectives, entering(): pieces = jax.tree.map(lambda part: lax.all_gather(part, axis), subtotal)  39 us
    all_to_all x1, blocking collectives, sent_and_summed(): lax.all_to_all(parts, axis, split_axis=0, concat_axis=0, tiled=True)  15.5 us
    add x6, other arithmetic, combine(): return (earlier[0] + later[0], earlier[1] + later[1])  10.1 us
    ppermute x1, waiting for transfers between devices, shifted(): return lax.ppermute(block, axis, route)  7.29 us
    all_to_all x1, blocking collectives, sent_to_all(): return lax.all_to_all(copies, axis, split_axis=0, concat_axis=0, tiled=True)  5.98 us
    dot_general x2, matrix products, taylor_features(): jnp.einsum('the,ef->thf', extended, jnp.asarray(right_table), precision=hp)  5.56 us
    dot_general x2, matrix products, taylor_features(): jnp.einsum('the,ef->thf', extended, jnp.asarray(left_table), precision=hp)  5.22 us
  transfers between devices with their start and end apart: 4, of which 3 were waited for; matrix products, arithmetic and copies ran while one was open for 4% of the time, Pallas kernels for 0%

commit v1 on v0

v1 whole, which is shorter than its diff:
```python
import math

import jax
import jax.numpy as jnp
from jax import lax
from jax.experimental import pallas as pl
from jax.experimental.pallas import tpu as pltpu
from jax.sharding import PartitionSpec as P

D = 2048
HALF = 1024
FD = 16
DV = 128
ROWS = 512
HALO = 16
PADDED = HALO + ROWS
HEADS = 8
FEAT = 160
TILE = 256
Z, Y, X = 8, 4, 4
BF = jnp.bfloat16
F32 = jnp.float32
MESH = pl.DeviceIdType.MESH
PAIR_ORDER = (2, 1, 3, 0)
Z_ORDER = (4, 3, 5, 2, 6, 1, 7)


def dot(a, b):
    return jnp.dot(a, b, preferred_element_type=F32)


def features(u):
    parts = [u * u * F32(1.0 / math.sqrt(2.0 * FD))]
    for distance in range(1, 8):
        parts.append(u * pltpu.roll(u, FD - distance, 0) * F32(1.0 / math.sqrt(FD)))
    parts.append(u[0:8] * u[8:16] * F32(1.0 / math.sqrt(FD)))
    parts.append(u * F32(FD ** (-0.25)))
    row = lax.broadcasted_iota(jnp.int32, (8, u.shape[1]), 0)
    parts.append(jnp.where(row == 0, F32(1.0), F32(0.0)))
    return jnp.concatenate(parts, 0)


def kernel(
    tok, wq, wk, wv, cq, ck, cv, wo, gn, out,
    xbuf, wqk, wvb, wob, cqb, ckb, cvb, gnb,
    acc, pbuf, qt, kt, vbuf, pk, pq, num,
    loc, recv1, cbuf, ltx, ry, ttx, rx, p3, recv3,
    ybuf, ttxo, trx, share, sqtx, sqrx, obuf,
    lsem, tok_s, tok_r, halo_s, halo_r, s1_s, s1_r, y_s, y_r, x_s, x_r, s3_s, s3_r, o_s, o_r, q_s, q_r,
):
    me = lax.axis_index("ctx")
    c = lax.axis_index("head")
    other = 1 - c
    z = lax.rem(me, Z)
    y = lax.rem(lax.div(me, Z), Y)
    x = lax.div(me, Z * Y)

    def z_peer(i):
        return me - z + lax.rem(z + i, Z)

    def y_peer(i):
        return me + (lax.rem(y + i, Y) - y) * Z

    def x_peer(i):
        return me + (lax.rem(x + i, X) - x) * (Z * Y)

    after = lax.rem(me + 1, Z * Y * X)
    before = lax.rem(me + Z * Y * X - 1, Z * Y * X)

    def remote(src, dst, send, recv, ctx, head):
        return pltpu.make_async_remote_copy(
            src_ref=src, dst_ref=dst, send_sem=send, recv_sem=recv,
            device_id={"ctx": ctx, "head": head}, device_id_type=MESH,
        )

    barrier = pltpu.get_barrier_semaphore()
    greeted = [(me, other), (before, c), (before, other)]
    greeted += [(z_peer(i), c) for i in range(1, Z)]
    greeted += [(y_peer(i), c) for i in range(1, Y)]
    greeted += [(x_peer(i), c) for i in range(1, X)]
    for ctx, head in greeted:
        pl.semaphore_signal(barrier, inc=1, device_id={"ctx": ctx, "head": head}, device_id_type=MESH)

    mine = pl.ds(pl.multiple_of(c * HALF, HALF), HALF)
    theirs = pl.ds(pl.multiple_of(other * HALF, HALF), HALF)
    tail_rows = pl.ds(HALO, ROWS)
    loads = [
        pltpu.make_async_copy(tok, xbuf.at[c, tail_rows], lsem.at[0]),
        pltpu.make_async_copy(wq, wqk.at[:, pl.ds(0, 128)], lsem.at[1]),
        pltpu.make_async_copy(wk, wqk.at[:, pl.ds(128, 128)], lsem.at[2]),
        pltpu.make_async_copy(wv.at[mine], wvb.at[mine], lsem.at[3]),
        pltpu.make_async_copy(wv.at[theirs], wvb.at[theirs], lsem.at[4]),
        pltpu.make_async_copy(cq, cqb, lsem.at[5]),
        pltpu.make_async_copy(ck, ckb, lsem.at[6]),
        pltpu.make_async_copy(cv, cvb, lsem.at[7]),
        pltpu.make_async_copy(gn, gnb, lsem.at[8]),
        pltpu.make_async_copy(wo, wob, lsem.at[9]),
    ]
    for copy in loads:
        copy.start()
    pl.semaphore_wait(barrier, len(greeted))

    last = tok.at[pl.ds(ROWS - HALO, HALO)]
    halos = [
        remote(last, xbuf.at[c, pl.ds(0, HALO)], halo_s.at[0], halo_r.at[c], after, c),
        remote(last, xbuf.at[c, pl.ds(0, HALO)], halo_s.at[1], halo_r.at[c], after, other),
    ]
    swap = remote(tok, xbuf.at[c, tail_rows], tok_s.at[0], tok_r.at[0], me, other)
    for copy in halos:
        copy.start()
    swap.start()

    def halo_in(half):
        remote(last, xbuf.at[half, pl.ds(0, HALO)], halo_s.at[0], halo_r.at[half], before, c).wait_recv()

    halo_in(c)
    for copy in loads[:4]:
        copy.wait()

    def columns(pair):
        return pl.ds(pl.multiple_of(pair * TILE, TILE), TILE)

    pairs = [lax.rem(lax.div(z, 2) + i, 4) for i in PAIR_ORDER]
    acc[0] = dot(xbuf[c], wqk[mine, :])
    for i, pair in enumerate(pairs):
        acc[1 + i] = dot(xbuf[c], wvb[mine, columns(pair)])
    halo_in(other)
    swap.wait_recv()
    for copy in loads[4:]:
        copy.wait()

    first_block = me == 0

    def convolved(taps):
        pbuf[8:16, :] = jnp.where(first_block, F32(0.0), pbuf[8:16, :])
        return (
            taps[0:1] * pbuf[16 : 16 + ROWS, :]
            + taps[1:2] * pbuf[15 : 15 + ROWS, :]
            + taps[2:3] * pbuf[14 : 14 + ROWS, :]
        )

    pbuf[...] = (acc[0] + dot(xbuf[other], wqk[theirs, :])).astype(BF).astype(F32)
    taps = jnp.concatenate([cqb[...].astype(F32), ckb[...].astype(F32)], 1)
    both = convolved(taps).T
    qt[...] = both[0:128]
    kt[...] = both[128:256]

    def key_head(h, value):
        feats = features(kt[pl.ds(pl.multiple_of(h * FD, FD), FD), :]).astype(BF)
        pk[h] = feats
        state = dot(feats, value)
        norm = lax.dot_general(
            jnp.ones((8, ROWS), BF), feats, (((1,), (1,)), ((), ())), preferred_element_type=F32
        )[0:1]
        norm = jnp.concatenate([norm, jnp.zeros((1, 256 - FEAT), F32)], 1)
        row = lax.broadcasted_iota(jnp.int32, (16, DV), 0)
        tail = state[144:160]
        tail = jnp.where(row == 9, norm[:, 0:128], tail)
        tail = jnp.where(row == 10, norm[:, 128:256], tail)
        return jnp.concatenate([state[0:144], tail], 0).astype(BF)

    sends1 = []
    for i, pair in enumerate(pairs):
        pbuf[...] = (acc[1 + i] + dot(xbuf[other], wvb[theirs, columns(pair)])).astype(BF).astype(F32)
        values = convolved(cvb[:, columns(pair)].astype(F32)).astype(BF)
        vbuf[pair] = values
        if PAIR_ORDER[i]:
            for b in range(2):
                slot = 2 * i + b
                loc[slot] = key_head(2 * pair + b, values[:, b * DV : (b + 1) * DV])
                sends1.append((slot, 2 * pair + b))
                slot, dest = sends1[-1]
                remote(loc.at[slot], recv1.at[z], s1_s.at[slot], s1_r.at[z], me - z + dest, c).start()
        else:
            half = lax.rem(z, 2)
            dest = 2 * pair + (1 - half)
            slot = 2 * i
            chosen = jnp.where(half == 0, values[:, DV:], values[:, :DV])
            loc[slot] = key_head(dest, chosen)
            sends1.append((slot, dest))
            remote(loc.at[slot], recv1.at[z], s1_s.at[slot], s1_r.at[z], me - z + dest, c).start()
            chosen = jnp.where(half == 0, values[:, :DV], values[:, DV:])
            recv1[z] = key_head(z, chosen)

    ones = jnp.ones((ROWS, DV), BF)

    def query_head(h):
        feats = features(qt[h * FD : (h + 1) * FD, :])
        pq[h] = jnp.concatenate([feats, jnp.zeros((256 - FEAT, ROWS), F32)], 0).T.astype(BF)
        value = vbuf[h // 2][:, (h % 2) * DV : (h % 2 + 1) * DV]
        value = jnp.concatenate([value, ones], 1)
        for t in range(ROWS // TILE):
            span = (t + 1) * TILE
            scores = dot(pq[h, t * TILE : span, 0:FEAT], pk[h, :, 0:span])
            row = lax.broadcasted_iota(jnp.int32, (TILE, span), 0) + t * TILE
            col = lax.broadcasted_iota(jnp.int32, (TILE, span), 1)
            scores = jnp.where(row >= col, scores, F32(0.0)).astype(BF)
            num[h, t * TILE : span] = dot(scores, value[0:span])

    for h in range(3):
        query_head(h)

    for i in range(1, Z):
        slot = lax.rem(z + Z - i, Z)
        remote(loc.at[0], recv1.at[slot], s1_s.at[0], s1_r.at[slot], z_peer(i), c).wait_recv()
    total = jnp.zeros((FEAT, DV), F32)
    for t in range(Z):
        cbuf[t] = total
        total = total + recv1[t].astype(F32)
    line = total.astype(BF)
    ltx[...] = line
    sends_y = [remote(ltx, ry.at[y], y_s.at[i], y_r.at[y], y_peer(i), c) for i in range(1, Y)]
    for copy in sends_y:
        copy.start()
    ry[y] = line

    for h in range(3, 5):
        query_head(h)

    for i in range(1, Y):
        slot = lax.rem(y + Y - i, Y)
        remote(ltx, ry.at[slot], y_s.at[0], y_r.at[slot], y_peer(i), c).wait_recv()
    offset = jnp.zeros((FEAT, DV), F32)
    total = jnp.zeros((FEAT, DV), F32)
    for t in range(Y):
        part = ry[t].astype(F32)
        total = total + part
        offset = offset + jnp.where(t < y, part, F32(0.0))
    plane = total.astype(BF)
    ttx[...] = plane
    sends_x = [remote(ttx, rx.at[x], x_s.at[i], x_r.at[x], x_peer(i), c) for i in range(1, X)]
    for copy in sends_x:
        copy.start()
    rx[x] = plane

    for h in range(5, 8):
        query_head(h)

    for i in range(1, X):
        slot = lax.rem(x + X - i, X)
        remote(ttx, rx.at[slot], x_s.at[0], x_r.at[slot], x_peer(i), c).wait_recv()
    for t in range(X):
        offset = offset + jnp.where(t < x, rx[t].astype(F32), F32(0.0))
    sends3 = []
    for i in Z_ORDER:
        dest = lax.rem(z + i, Z)
        p3[i] = (cbuf[dest] + offset).astype(BF)
        sends3.append(remote(p3.at[i], recv3.at[z], s3_s.at[i], s3_r.at[z], me - z + dest, c))
        sends3[-1].start()
    recv3[z] = (cbuf[z] + offset).astype(BF)

    def finish_head(h):
        state = recv3[h]
        tail = state[144:160].astype(F32)
        norm = jnp.concatenate([tail[9:10], tail[10:11]], 1)
        norm = jnp.broadcast_to(norm, (128, 256)).T[0:FEAT].astype(BF)
        sums = dot(pq[h][:, 0:FEAT], jnp.concatenate([state, norm], 1)) + num[h]
        ybuf[:, pl.ds(pl.multiple_of(h * DV, DV), DV)] = (sums[:, :DV] / sums[:, DV:]).astype(BF)

    finish_head(z)
    for i in Z_ORDER:
        slot = lax.rem(z + Z - i, Z)
        remote(p3.at[i], recv3.at[slot], s3_s.at[i], s3_r.at[slot], z_peer(i), c).wait_recv()
        finish_head(slot)

    sends_o = []
    for n in range(HALF // TILE):
        cols = pl.ds(pl.multiple_of(other * HALF + n * TILE, TILE), TILE)
        ttxo[n] = dot(ybuf[...], wob[:, cols]).astype(BF)
        sends_o.append(remote(ttxo.at[n], trx.at[n], o_s.at[n], o_r.at[n], me, other))
        sends_o[-1].start()
    squares = jnp.zeros((ROWS, 128), F32)
    for n in range(HALF // TILE):
        cols = pl.ds(pl.multiple_of(c * HALF + n * TILE, TILE), TILE)
        term = dot(ybuf[...], wob[:, cols])
        sends_o[n].wait_recv()
        term = term + trx[n].astype(F32)
        share[n] = term
        squares = squares + term[:, :128] * term[:, :128] + term[:, 128:] * term[:, 128:]
    sqtx[...] = squares
    send_q = remote(sqtx, sqrx, q_s.at[0], q_r.at[0], me, other)
    send_q.start()
    send_q.wait_recv()
    mean = jnp.sum(sqtx[...] + sqrx[...], 1, keepdims=True) * F32(1.0 / D)
    scale = lax.rsqrt(mean + F32(1e-05))
    stores = []
    for n in range(HALF // TILE):
        cols = pl.ds(n * TILE, TILE)
        obuf[:, cols] = (share[n] * scale * gnb[:, cols].astype(F32)).astype(BF)
        stores.append(pltpu.make_async_copy(obuf.at[:, cols], out.at[:, cols], lsem.at[n]))
        stores[-1].start()

    for copy in halos:
        copy.wait_send()
    swap.wait_send()
    for slot, dest in sends1:
        remote(loc.at[slot], recv1.at[z], s1_s.at[slot], s1_r.at[z], me - z + dest, c).wait_send()
    for copy in sends_y + sends_x + sends3 + sends_o + [send_q]:
        copy.wait_send()
    for copy in stores:
        copy.wait()


def body(tokens, w_query, w_key, w_value, conv_query, conv_key, conv_value, w_out, gain):
    dma = pltpu.SemaphoreType.DMA
    vm = pltpu.VMEM
    return pl.pallas_call(
        kernel,
        out_shape=jax.ShapeDtypeStruct((ROWS, HALF), BF),
        in_specs=[pl.BlockSpec(memory_space=pl.ANY)] * 9,
        out_specs=pl.BlockSpec(memory_space=pl.ANY),
        scratch_shapes=[
            vm((2, PADDED, HALF), BF), vm((D, 256), BF), vm((D, HALF), BF), vm((HALF, D), BF),
            vm((3, 128), BF), vm((3, 128), BF), vm((3, HALF), BF), vm((1, HALF), BF),
            vm((5, PADDED, TILE), F32), vm((PADDED, TILE), F32), vm((128, ROWS), F32), vm((128, ROWS), F32),
            vm((4, ROWS, TILE), BF), vm((HEADS, FEAT, ROWS), BF), vm((HEADS, ROWS, 256), BF),
            vm((HEADS, ROWS, TILE), F32),
            vm((8, FEAT, DV), BF), vm((Z, FEAT, DV), BF), vm((Z, FEAT, DV), F32), vm((FEAT, DV), BF),
            vm((Y, FEAT, DV), BF), vm((FEAT, DV), BF), vm((X, FEAT, DV), BF), vm((Z, FEAT, DV), BF),
            vm((Z, FEAT, DV), BF),
            vm((ROWS, HALF), BF), vm((4, ROWS, TILE), BF), vm((4, ROWS, TILE), BF), vm((4, ROWS, TILE), F32),
            vm((ROWS, 128), F32), vm((ROWS, 128), F32), vm((ROWS, HALF), BF),
            dma((10,)), dma((1,)), dma((1,)), dma((2,)), dma((2,)), dma((8,)), dma((8,)), dma((4,)), dma((4,)),
            dma((4,)), dma((4,)), dma((8,)), dma((8,)), dma((4,)), dma((4,)), dma((1,)), dma((1,)),
        ],
        compiler_params=pltpu.CompilerParams(
            collective_id=0, has_side_effects=True, vmem_limit_bytes=58 * 1024 * 1024
        ),
    )(tokens, w_query, w_key, w_value, conv_query, conv_key, conv_value, w_out, gain.reshape(1, HALF))


def solution(mesh):
    return jax.shard_map(
        body,
        mesh=mesh,
        in_specs=(
            P("ctx", "head"),
            P(None, "head"),
            P(None, "head"),
            P(None, "head"),
            P(None, "head"),
            P(None, "head"),
            P(None, "head"),
            P("head", None),
            P("head"),
        ),
        out_specs=P("ctx", "head"),
        check_vma=False,
    )
```

time: 236 us -> 54.6 us (0.23)
  the two profiles are of different devices: /device:TPU:5 before, /device:TPU:1 now
where the time goes in v1:
time: 54.6 us; the launch traced here: 54.5 us
  Pallas kernels  50.9 us (93%)
  local copies, waits for them, and re-layouts  3.54 us (6%)
    pallas_call x1, Pallas kernels, body(): pl.pallas_call(kernel, out_shape=jax.ShapeDtypeStruct((ROWS, HALF), BF),...  50.9 us
    unnamed x1, local copies, waits for them, and re-layouts  2.26 us
    reshape x1, local copies, waits for them, and re-layouts, body(): gain.reshape(1, HALF)  1.28 us

profile of v1, /device:TPU:1, one launch (start us, length us, event | category | flops | bytes accessed | tf_op | source)
XLA Modules:
  0.0 54.5 jit_solution(5078098755149595726)
XLA Ops:
  0.0 1.3 %reshape.3.gn = bf16[1,1024]{1,0:T(2,128)(2,1)} reshape(bf16[1024]{0:T(1024)(128)(2,1)} %param.17) | data formatting | bytes 4096 | tf_op jit(solution)/shard_map/reshape | solution.py:329
  1.3 50.9 %shard_map.91 = bf16[512,1024]{1,0:T(8,128)(2,1)} custom-call(bf16[512,1024]{1,0:T(8,128)(2,1)} %tok.1, bf16[2048,128]{1,0:T(8,128)(2,1)} %wq.1, bf16[2048,128]{1,0:T(8,128)(2,1)} %wk.1, bf16[2048,1024]{1,0:T(8,128)(2,1)} %wv.1, bf16[3,128]{1,0:T(4,128)(2,1)} %cq.1, bf16[3,128]{1,0:T(4,128)(2,1)} %ck.1, bf16[3,1024]{1,0:T(4,128)(2,1)} %cv.1, ...), custom_call_target="tpu_custom_call" | custom-call | tf_op jit(solution)/shard_map/pallas_call | solution.py:307
  52.2 2.3 %copy.11 = bf16[512,1024]{1,0:T(8,128)(2,1)} copy(bf16[512,1024]{1,0:T(8,128)(2,1)} %shard_map.91) | data formatting | bytes 2097152

commit v2 on v1

v2 whole, which is shorter than its diff:
```python
import math

import jax
import jax.numpy as jnp
from jax import lax
from jax.experimental import pallas as pl
from jax.experimental.pallas import tpu as pltpu
from jax.sharding import PartitionSpec as P

D = 2048
HALF = 1024
FD = 16
DV = 128
ROWS = 512
HALO = 16
PADDED = HALO + ROWS
HEADS = 8
FEAT = 160
TILE = 256
Z, Y, X = 8, 4, 4
BF = jnp.bfloat16
F32 = jnp.float32
MESH = pl.DeviceIdType.MESH
PLANE = X * Y
CHUNK = FEAT // 2
PAIR_ORDER = (2, 1, 3, 0)
Z_ORDER = (4, 3, 5, 2, 6, 1, 7)


def dot(a, b):
    return jnp.dot(a, b, preferred_element_type=F32)


def features(u):
    parts = [u * u * F32(1.0 / math.sqrt(2.0 * FD))]
    for distance in range(1, 8):
        parts.append(u * pltpu.roll(u, FD - distance, 0) * F32(1.0 / math.sqrt(FD)))
    parts.append(u[0:8] * u[8:16] * F32(1.0 / math.sqrt(FD)))
    parts.append(u * F32(FD ** (-0.25)))
    row = lax.broadcasted_iota(jnp.int32, (8, u.shape[1]), 0)
    parts.append(jnp.where(row == 0, F32(1.0), F32(0.0)))
    return jnp.concatenate(parts, 0)


def kernel(
    tok, wq, wk, wv, cq, ck, cv, wo, gn, out,
    xbuf, wqk, wvb, wob, cqb, ckb, cvb, gnb,
    acc, pbuf, qt, kt, vbuf, pk, pq, num,
    loc, recv1, cbuf, ltx, lrx, offset, p3, recv3,
    acc_out, ttxo, trx, share, sqtx, sqrx,
    lsem, tok_s, tok_r, halo_s, halo_r, s1_s, s1_r, l_s, l_r, s3_s, s3_r, o_s, o_r, q_s, q_r,
):
    me = lax.axis_index("ctx")
    c = lax.axis_index("head")
    other = 1 - c
    z = lax.rem(me, Z)
    line = lax.div(me, Z)

    def z_peer(i):
        return me - z + lax.rem(z + i, Z)

    def line_peer(i):
        return lax.rem(line + i + PLANE, PLANE) * Z + z

    after = lax.rem(me + 1, Z * Y * X)
    before = lax.rem(me + Z * Y * X - 1, Z * Y * X)

    def remote(src, dst, send, recv, ctx, head):
        return pltpu.make_async_remote_copy(
            src_ref=src, dst_ref=dst, send_sem=send, recv_sem=recv,
            device_id={"ctx": ctx, "head": head}, device_id_type=MESH,
        )

    barrier = pltpu.get_barrier_semaphore()
    greeted = [(me, other), (before, c), (before, other)]
    greeted += [(z_peer(i), c) for i in range(1, Z)]
    greeted += [(line_peer(i), c) for i in range(1, PLANE)]
    for ctx, head in greeted:
        pl.semaphore_signal(barrier, inc=1, device_id={"ctx": ctx, "head": head}, device_id_type=MESH)

    mine = pl.ds(pl.multiple_of(c * HALF, HALF), HALF)
    theirs = pl.ds(pl.multiple_of(other * HALF, HALF), HALF)
    tail_rows = pl.ds(HALO, ROWS)
    loads = [
        pltpu.make_async_copy(tok, xbuf.at[c, tail_rows], lsem.at[0]),
        pltpu.make_async_copy(wq, wqk.at[:, pl.ds(0, 128)], lsem.at[1]),
        pltpu.make_async_copy(wk, wqk.at[:, pl.ds(128, 128)], lsem.at[2]),
        pltpu.make_async_copy(wv.at[mine], wvb.at[mine], lsem.at[3]),
        pltpu.make_async_copy(wv.at[theirs], wvb.at[theirs], lsem.at[4]),
        pltpu.make_async_copy(cq, cqb, lsem.at[5]),
        pltpu.make_async_copy(ck, ckb, lsem.at[6]),
        pltpu.make_async_copy(cv, cvb, lsem.at[7]),
        pltpu.make_async_copy(gn, gnb, lsem.at[8]),
        pltpu.make_async_copy(wo, wob, lsem.at[9]),
    ]
    for copy in loads:
        copy.start()
    pl.semaphore_wait(barrier, len(greeted))

    last = tok.at[pl.ds(ROWS - HALO, HALO)]
    halos = [
        remote(last, xbuf.at[c, pl.ds(0, HALO)], halo_s.at[0], halo_r.at[c], after, c),
        remote(last, xbuf.at[c, pl.ds(0, HALO)], halo_s.at[1], halo_r.at[c], after, other),
    ]
    swap = remote(tok, xbuf.at[c, tail_rows], tok_s.at[0], tok_r.at[0], me, other)
    swap.start()

    @pl.when(me < Z * PLANE - 1)
    def _():
        for copy in halos:
            copy.start()

    def halo_in(half):
        rows = xbuf.at[half, pl.ds(0, HALO)]

        @pl.when(me > 0)
        def _():
            remote(last, rows, halo_s.at[0], halo_r.at[half], before, c).wait_recv()

        @pl.when(me == 0)
        def _():
            rows[...] = jnp.zeros((HALO, HALF), BF)

    halo_in(c)
    for copy in loads[:4]:
        copy.wait()

    def columns(pair):
        return pl.ds(pl.multiple_of(pair * TILE, TILE), TILE)

    pairs = [lax.rem(lax.div(z, 2) + i, 4) for i in PAIR_ORDER]
    acc[0] = dot(xbuf[c], wqk[mine, :])
    for i, pair in enumerate(pairs):
        acc[1 + i] = dot(xbuf[c], wvb[mine, columns(pair)])
    halo_in(other)
    swap.wait_recv()
    for copy in loads[4:]:
        copy.wait()

    def convolved(taps):
        return (
            taps[0:1] * pbuf[16 : 16 + ROWS, :]
            + taps[1:2] * pbuf[15 : 15 + ROWS, :]
            + taps[2:3] * pbuf[14 : 14 + ROWS, :]
        )

    pbuf[...] = (acc[0] + dot(xbuf[other], wqk[theirs, :])).astype(BF).astype(F32)
    taps = jnp.concatenate([cqb[...].astype(F32), ckb[...].astype(F32)], 1)
    both = convolved(taps).T
    qt[...] = both[0:128]
    kt[...] = both[128:256]

    def key_head(h, value):
        feats = features(kt[pl.ds(pl.multiple_of(h * FD, FD), FD), :]).astype(BF)
        pk[h] = feats
        state = dot(feats, value)
        norm = lax.dot_general(
            jnp.ones((8, ROWS), BF), feats, (((1,), (1,)), ((), ())), preferred_element_type=F32
        )[0:1]
        norm = jnp.concatenate([norm, jnp.zeros((1, 256 - FEAT), F32)], 1)
        row = lax.broadcasted_iota(jnp.int32, (16, DV), 0)
        tail = state[144:160]
        tail = jnp.where(row == 9, norm[:, 0:128], tail)
        tail = jnp.where(row == 10, norm[:, 128:256], tail)
        return jnp.concatenate([state[0:144], tail], 0).astype(BF)

    def rows_of(chunk):
        return pl.ds(chunk * CHUNK, CHUNK)

    sends1 = []

    def state_out(slot, dest, chunk):
        rows = rows_of(chunk)
        sends1.append(
            remote(
                loc.at[slot, rows], recv1.at[z, rows], s1_s.at[chunk, slot], s1_r.at[chunk, z], me - z + dest, c
            )
        )
        sends1[-1].start()

    routed = []
    for i, pair in enumerate(pairs):
        pbuf[...] = (acc[1 + i] + dot(xbuf[other], wvb[theirs, columns(pair)])).astype(BF).astype(F32)
        values = convolved(cvb[:, columns(pair)].astype(F32)).astype(BF)
        vbuf[pair] = values
        if PAIR_ORDER[i]:
            for b in range(2):
                slot, dest = 2 * i + b, 2 * pair + b
                loc[slot] = key_head(dest, values[:, b * DV : (b + 1) * DV])
                routed.append((slot, dest))
                state_out(slot, dest, 0)
        else:
            half = lax.rem(z, 2)
            slot, dest = 2 * i, 2 * pair + (1 - half)
            loc[slot] = key_head(dest, jnp.where(half == 0, values[:, DV:], values[:, :DV]))
            routed.append((slot, dest))
            state_out(slot, dest, 0)
    for slot, dest in routed:
        state_out(slot, dest, 1)
    half = lax.rem(z, 2)
    recv1[z] = key_head(z, jnp.where(half == 0, values[:, :DV], values[:, DV:]))

    ones = jnp.ones((ROWS, DV), BF)

    def query_head(h):
        feats = features(qt[h * FD : (h + 1) * FD, :])
        pq[h] = jnp.concatenate([feats, jnp.zeros((256 - FEAT, ROWS), F32)], 0).T.astype(BF)
        value = vbuf[h // 2][:, (h % 2) * DV : (h % 2 + 1) * DV]
        value = jnp.concatenate([value, ones], 1)
        for t in range(ROWS // TILE):
            span = (t + 1) * TILE
            scores = dot(pq[h, t * TILE : span, 0:FEAT], pk[h, :, 0:span])
            row = lax.broadcasted_iota(jnp.int32, (TILE, span), 0) + t * TILE
            col = lax.broadcasted_iota(jnp.int32, (TILE, span), 1)
            scores = jnp.where(row >= col, scores, F32(0.0)).astype(BF)
            num[h, t * TILE : span] = dot(scores, value[0:span])

    def line_send(chunk, i):
        rows = rows_of(chunk)
        return remote(
            ltx.at[rows], lrx.at[i, rows], l_s.at[chunk, i], l_r.at[chunk, i], line_peer(i), c
        )

    def line_totals(chunk):
        rows = rows_of(chunk)
        for i in range(1, Z):
            slot = lax.rem(z + Z - i, Z)
            remote(
                loc.at[0, rows], recv1.at[slot, rows], s1_s.at[chunk, 0], s1_r.at[chunk, slot], z_peer(i), c
            ).wait_recv()
        total = jnp.zeros((CHUNK, DV), F32)
        for t in range(Z):
            cbuf[t, rows] = total
            total = total + recv1[t, rows].astype(F32)
        ltx[rows] = total.astype(BF)
        for i in range(1, PLANE):

            @pl.when(line + i < PLANE)
            def _():
                line_send(chunk, i).start()

    sends3 = []

    def prefixes(chunk):
        rows = rows_of(chunk)
        offset[rows] = jnp.zeros((CHUNK, DV), F32)
        for i in range(1, PLANE):

            @pl.when(line >= i)
            def _():
                line_send(chunk, i).wait_recv()
                offset[rows] += lrx[i, rows].astype(F32)

        for i in Z_ORDER:
            dest = lax.rem(z + i, Z)
            p3[i, rows] = (cbuf[dest, rows] + offset[rows]).astype(BF)
            sends3.append(
                remote(p3.at[i, rows], recv3.at[z, rows], s3_s.at[chunk, i], s3_r.at[chunk, z], me - z + dest, c)
            )
            sends3[-1].start()
        recv3[z, rows] = (cbuf[z, rows] + offset[rows]).astype(BF)

    for h in range(6):
        query_head(h)
    line_totals(0)
    query_head(6)
    line_totals(1)
    query_head(7)
    prefixes(0)
    prefixes(1)

    def finished_head(h):
        state = recv3[h]
        tail = state[144:160].astype(F32)
        norm = jnp.concatenate([tail[9:10], tail[10:11]], 1)
        norm = jnp.broadcast_to(norm, (128, 256)).T[0:FEAT].astype(BF)
        sums = dot(pq[h][:, 0:FEAT], jnp.concatenate([state, norm], 1)) + num[h]
        return (sums[:, :DV] / sums[:, DV:]).astype(BF)

    def arrived_head(i):
        if i == 0:
            return z
        slot = lax.rem(z + Z - i, Z)
        for chunk in range(2):
            rows = rows_of(chunk)
            remote(
                p3.at[i, rows], recv3.at[slot, rows], s3_s.at[chunk, i], s3_r.at[chunk, slot], z_peer(i), c
            ).wait_recv()
        return slot

    def head_rows(h):
        return pl.ds(pl.multiple_of(h * DV, DV), DV)

    order = (0,) + Z_ORDER
    sends_o = []
    for step in range(4):
        heads = [arrived_head(order[2 * step])]
        left = finished_head(heads[0])
        heads.append(arrived_head(order[2 * step + 1]))
        attended = jnp.concatenate([left, finished_head(heads[1])], 1)

        def term(start, n):
            cols = pl.ds(pl.multiple_of(start * HALF + n * TILE, TILE), TILE)
            weights = jnp.concatenate([wob[head_rows(h), cols] for h in heads], 0)
            return dot(attended, weights)

        if step < 3:
            for k, start in enumerate((other, c)):
                for n in range(HALF // TILE):
                    new = term(start, n)
                    acc_out[k, n] = new if step == 0 else acc_out[k, n] + new
        else:
            for n in range(HALF // TILE):
                ttxo[n] = (acc_out[0, n] + term(other, n)).astype(BF)
                sends_o.append(remote(ttxo.at[n], trx.at[n], o_s.at[n], o_r.at[n], me, other))
                sends_o[-1].start()
    squares = jnp.zeros((ROWS, 128), F32)
    for n in range(HALF // TILE):
        mixed = acc_out[1, n] + term(c, n)
        sends_o[n].wait_recv()
        mixed = mixed + trx[n].astype(F32)
        share[n] = mixed
        squares = squares + mixed[:, :128] * mixed[:, :128] + mixed[:, 128:] * mixed[:, 128:]
    sqtx[...] = squares
    send_q = remote(sqtx, sqrx, q_s.at[0], q_r.at[0], me, other)
    send_q.start()
    send_q.wait_recv()
    mean = jnp.sum(sqtx[...] + sqrx[...], 1, keepdims=True) * F32(1.0 / D)
    scale = lax.rsqrt(mean + F32(1e-05))
    for n in range(HALF // TILE):
        gains = jnp.concatenate([gnb[2 * n : 2 * n + 1], gnb[2 * n + 1 : 2 * n + 2]], 1).astype(F32)
        out[:, n * TILE : (n + 1) * TILE] = (share[n] * scale * gains).astype(BF)

    @pl.when(me < Z * PLANE - 1)
    def _():
        for copy in halos:
            copy.wait_send()

    swap.wait_send()
    for copy in sends1 + sends3 + sends_o + [send_q]:
        copy.wait_send()
    for chunk in range(2):
        for i in range(1, PLANE):

            @pl.when(line + i < PLANE)
            def _():
                line_send(chunk, i).wait_send()


def body(tokens, w_query, w_key, w_value, conv_query, conv_key, conv_value, w_out, gain):
    dma = pltpu.SemaphoreType.DMA
    vm = pltpu.VMEM
    return pl.pallas_call(
        kernel,
        out_shape=pltpu.VMEM((ROWS, HALF), BF),
        in_specs=[pl.BlockSpec(memory_space=pl.ANY)] * 9,
        out_specs=pl.BlockSpec(memory_space=pltpu.VMEM),
        scratch_shapes=[
            vm((2, PADDED, HALF), BF), vm((D, 256), BF), vm((D, HALF), BF), vm((HALF, D), BF),
            vm((3, 128), BF), vm((3, 128), BF), vm((3, HALF), BF), vm((8, 128), BF),
            vm((5, PADDED, TILE), F32), vm((PADDED, TILE), F32), vm((128, ROWS), F32), vm((128, ROWS), F32),
            vm((4, ROWS, TILE), BF), vm((HEADS, FEAT, ROWS), BF), vm((HEADS, ROWS, 256), BF),
            vm((HEADS, ROWS, TILE), F32),
            vm((8, FEAT, DV), BF), vm((Z, FEAT, DV), BF), vm((Z, FEAT, DV), F32), vm((FEAT, DV), BF),
            vm((PLANE, FEAT, DV), BF), vm((FEAT, DV), F32), vm((Z, FEAT, DV), BF), vm((Z, FEAT, DV), BF),
            vm((2, 4, ROWS, TILE), F32), vm((4, ROWS, TILE), BF), vm((4, ROWS, TILE), BF), vm((4, ROWS, TILE), F32),
            vm((ROWS, 128), F32), vm((ROWS, 128), F32),
            dma((10,)), dma((1,)), dma((1,)), dma((2,)), dma((2,)), dma((2, 8)), dma((2, 8)),
            dma((2, PLANE)), dma((2, PLANE)), dma((2, 8)), dma((2, 8)), dma((4,)), dma((4,)), dma((1,)), dma((1,)),
        ],
        compiler_params=pltpu.CompilerParams(
            collective_id=0, has_side_effects=True, vmem_limit_bytes=58 * 1024 * 1024
        ),
    )(tokens, w_query, w_key, w_value, conv_query, conv_key, conv_value, w_out, gain.reshape(8, 128))


def solution(mesh):
    return jax.shard_map(
        body,
        mesh=mesh,
        in_specs=(
            P("ctx", "head"),
            P(None, "head"),
            P(None, "head"),
            P(None, "head"),
            P(None, "head"),
            P(None, "head"),
            P(None, "head"),
            P("head", None),
            P("head"),
        ),
        out_specs=P("ctx", "head"),
        check_vma=False,
    )
```

time: 54.6 us -> 48.1 us (0.88)
  the two profiles are of different devices: /device:TPU:1 before, /device:TPU:5 now
where the time goes in v2:
time: 48.1 us; the launch traced here: 48 us
  Pallas kernels  47 us (98%)
  local copies, waits for them, and re-layouts  0.97 us (2%)
    pallas_call x1, Pallas kernels, body(): pl.pallas_call(kernel, out_shape=pltpu.VMEM((ROWS, HALF), BF), in_specs=[...  47 us
    unnamed x1, local copies, waits for them, and re-layouts  0.97 us

profile of v2, /device:TPU:5, one launch (start us, length us, event | category | flops | bytes accessed | tf_op | source)
XLA Modules:
  0.0 48.0 jit_solution(2772130633062523377)
XLA Ops:
  0.0 47.0 %shard_map.91 = bf16[512,1024]{1,0:T(8,128)(2,1)S(1)} custom-call(bf16[512,1024]{1,0:T(8,128)(2,1)} %tok.1, bf16[2048,128]{1,0:T(8,128)(2,1)} %wq.1, bf16[2048,128]{1,0:T(8,128)(2,1)} %wk.1, bf16[2048,1024]{1,0:T(8,128)(2,1)} %wv.1, bf16[3,128]{1,0:T(4,128)(2,1)} %cq.1, bf16[3,128]{1,0:T(4,128)(2,1)} %ck.1, bf16[3,1024]{1,0:T(4,128)(2,1)} %cv.1, ...), custom_call_target="tpu_custom_call" | custom-call | tf_op jit(solution)/shard_map/pallas_call | solution.py:353
  47.0 1.0 %copy.11 = bf16[512,1024]{1,0:T(8,128)(2,1)} copy(bf16[512,1024]{1,0:T(8,128)(2,1)S(1)} %shard_map.91) | data formatting | bytes 2097152

commit v3 on v2

--- a/solution.py
+++ b/solution.py
@@ -17,12 +17,13 @@
 HEADS = 8
 FEAT = 160
 TILE = 256
+SPLIT = 256
 Z, Y, X = 8, 4, 4
 BF = jnp.bfloat16
 F32 = jnp.float32
 MESH = pl.DeviceIdType.MESH
 PLANE = X * Y
-CHUNK = FEAT // 2
+CHUNKS = ((0, 48), (48, 48), (96, 32), (128, 32))
 PAIR_ORDER = (2, 1, 3, 0)
 Z_ORDER = (4, 3, 5, 2, 6, 1, 7)
 
@@ -47,8 +48,8 @@
     xbuf, wqk, wvb, wob, cqb, ckb, cvb, gnb,
     acc, pbuf, qt, kt, vbuf, pk, pq, num,
     loc, recv1, cbuf, ltx, lrx, offset, p3, recv3,
-    acc_out, ttxo, trx, share, sqtx, sqrx,
-    lsem, tok_s, tok_r, halo_s, halo_r, s1_s, s1_r, l_s, l_r, s3_s, s3_r, o_s, o_r, q_s, q_r,
+    acc_out, ybuf, yrx, otx, gains,
+    lsem, tok_s, tok_r, halo_s, halo_r, s1_s, s1_r, l_s, l_r, s3_s, s3_r, w_s, w_r, g_s, g_r, o_s, o_r, f_s, f_r, ready,
 ):
     me = lax.axis_index("ctx")
     c = lax.axis_index("head")
@@ -72,11 +73,23 @@
         )
 
     barrier = pltpu.get_barrier_semaphore()
-    greeted = [(me, other), (before, c), (before, other)]
-    greeted += [(z_peer(i), c) for i in range(1, Z)]
-    greeted += [(line_peer(i), c) for i in range(1, PLANE)]
-    for ctx, head in greeted:
-        pl.semaphore_signal(barrier, inc=1, device_id={"ctx": ctx, "head": head}, device_id_type=MESH)
+    def greet(semaphore, ctx, head):
+        pl.semaphore_signal(semaphore, inc=1, device_id={"ctx": ctx, "head": head}, device_id_type=MESH)
+
+    greet(barrier, me, other)
+    for i in range(1, Z):
+        greet(barrier, z_peer(i), c)
+
+    @pl.when(me > 0)
+    def _():
+        greet(barrier, before, c)
+        greet(barrier, before, other)
+
+    for i in range(1, PLANE):
+
+        @pl.when(line + i < PLANE)
+        def _():
+            greet(barrier, line_peer(i), c)
 
     mine = pl.ds(pl.multiple_of(c * HALF, HALF), HALF)
     theirs = pl.ds(pl.multiple_of(other * HALF, HALF), HALF)
@@ -91,11 +104,11 @@
         pltpu.make_async_copy(ck, ckb, lsem.at[6]),
         pltpu.make_async_copy(cv, cvb, lsem.at[7]),
         pltpu.make_async_copy(gn, gnb, lsem.at[8]),
-        pltpu.make_async_copy(wo, wob, lsem.at[9]),
+        pltpu.make_async_copy(wo, wob.at[mine], lsem.at[9]),
     ]
     for copy in loads:
         copy.start()
-    pl.semaphore_wait(barrier, len(greeted))
+    pl.semaphore_wait(barrier, Z + line + jnp.where(me < Z * PLANE - 1, 2, 0))
 
     last = tok.at[pl.ds(ROWS - HALO, HALO)]
     halos = [
@@ -110,6 +123,12 @@
         for copy in halos:
             copy.start()
 
+    for i in range(1, PLANE):
+
+        @pl.when(line >= i)
+        def _():
+            greet(ready, line_peer(-i), c)
+
     def halo_in(half):
         rows = xbuf.at[half, pl.ds(0, HALO)]
 
@@ -134,8 +153,13 @@
         acc[1 + i] = dot(xbuf[c], wvb[mine, columns(pair)])
     halo_in(other)
     swap.wait_recv()
-    for copy in loads[4:]:
+    weights_out = remote(wo, wob.at[mine], w_s.at[0], w_r.at[0], me, other)
+    weights_out.start()
+    for copy in loads[4:9]:
         copy.wait()
+    gains[c] = gnb[...].astype(F32)
+    send_gains = remote(gains.at[c], gains.at[c], g_s.at[0], g_r.at[0], me, other)
+    send_gains.start()
 
     def convolved(taps):
         return (
@@ -165,7 +189,7 @@
         return jnp.concatenate([state[0:144], tail], 0).astype(BF)
 
     def rows_of(chunk):
-        return pl.ds(chunk * CHUNK, CHUNK)
+        return pl.ds(*CHUNKS[chunk])
 
     sends1 = []
 
@@ -189,14 +213,18 @@
                 loc[slot] = key_head(dest, values[:, b * DV : (b + 1) * DV])
                 routed.append((slot, dest))
                 state_out(slot, dest, 0)
+            for slot, dest in routed[-2:]:
+                state_out(slot, dest, 1)
         else:
             half = lax.rem(z, 2)
             slot, dest = 2 * i, 2 * pair + (1 - half)
             loc[slot] = key_head(dest, jnp.where(half == 0, values[:, DV:], values[:, :DV]))
             routed.append((slot, dest))
             state_out(slot, dest, 0)
-    for slot, dest in routed:
-        state_out(slot, dest, 1)
+            state_out(slot, dest, 1)
+    for chunk in range(2, len(CHUNKS)):
+        for slot, dest in routed:
+            state_out(slot, dest, chunk)
     half = lax.rem(z, 2)
     recv1[z] = key_head(z, jnp.where(half == 0, values[:, :DV], values[:, DV:]))
 
@@ -228,11 +256,17 @@
             remote(
                 loc.at[0, rows], recv1.at[slot, rows], s1_s.at[chunk, 0], s1_r.at[chunk, slot], z_peer(i), c
             ).wait_recv()
-        total = jnp.zeros((CHUNK, DV), F32)
+        total = jnp.zeros((CHUNKS[chunk][1], DV), F32)
         for t in range(Z):
             cbuf[t, rows] = total
             total = total + recv1[t, rows].astype(F32)
         ltx[rows] = total.astype(BF)
+        if chunk == 0:
+
+            @pl.when(line < PLANE - 1)
+            def _():
+                pl.semaphore_wait(ready, PLANE - 1 - line)
+
         for i in range(1, PLANE):
 
             @pl.when(line + i < PLANE)
@@ -243,7 +277,7 @@
 
     def prefixes(chunk):
         rows = rows_of(chunk)
-        offset[rows] = jnp.zeros((CHUNK, DV), F32)
+        offset[rows] = jnp.zeros((CHUNKS[chunk][1], DV), F32)
         for i in range(1, PLANE):
 
             @pl.when(line >= i)
@@ -266,8 +300,10 @@
     query_head(6)
     line_totals(1)
     query_head(7)
-    prefixes(0)
-    prefixes(1)
+    line_totals(2)
+    line_totals(3)
+    for chunk in range(len(CHUNKS)):
+        prefixes(chunk)
 
     def finished_head(h):
         state = recv3[h]
@@ -281,55 +317,51 @@
         if i == 0:
             return z
         slot = lax.rem(z + Z - i, Z)
-        for chunk in range(2):
+        for chunk in range(len(CHUNKS)):
             rows = rows_of(chunk)
             remote(
                 p3.at[i, rows], recv3.at[slot, rows], s3_s.at[chunk, i], s3_r.at[chunk, slot], z_peer(i), c
             ).wait_recv()
         return slot
 
-    def head_rows(h):
-        return pl.ds(pl.multiple_of(h * DV, DV), DV)
-
-    order = (0,) + Z_ORDER
-    sends_o = []
-    for step in range(4):
-        heads = [arrived_head(order[2 * step])]
-        left = finished_head(heads[0])
-        heads.append(arrived_head(order[2 * step + 1]))
-        attended = jnp.concatenate([left, finished_head(heads[1])], 1)
-
-        def term(start, n):
-            cols = pl.ds(pl.multiple_of(start * HALF + n * TILE, TILE), TILE)
-            weights = jnp.concatenate([wob[head_rows(h), cols] for h in heads], 0)
-            return dot(attended, weights)
-
-        if step < 3:
-            for k, start in enumerate((other, c)):
-                for n in range(HALF // TILE):
-                    new = term(start, n)
-                    acc_out[k, n] = new if step == 0 else acc_out[k, n] + new
-        else:
-            for n in range(HALF // TILE):
-                ttxo[n] = (acc_out[0, n] + term(other, n)).astype(BF)
-                sends_o.append(remote(ttxo.at[n], trx.at[n], o_s.at[n], o_r.at[n], me, other))
-                sends_o[-1].start()
-    squares = jnp.zeros((ROWS, 128), F32)
+    kept = pl.ds(pl.multiple_of(c * SPLIT, SPLIT), SPLIT)
+    given = pl.ds(pl.multiple_of(other * SPLIT, SPLIT), SPLIT)
+    sends_y = []
+    for i in range(HEADS):
+        h = arrived_head(((0,) + Z_ORDER)[i])
+        lanes = pl.ds(pl.multiple_of(h * DV, DV), DV)
+        ybuf[:, lanes] = finished_head(h)
+        sends_y.append(remote(ybuf.at[given, lanes], yrx.at[:, lanes], o_s.at[i], o_r.at[i], me, other))
+        sends_y[i].start()
+    loads[9].wait()
+    for n in range(D // TILE):
+        acc_out[n] = dot(ybuf[kept, :], wob[mine, n * TILE : (n + 1) * TILE])
+    weights_out.wait_recv()
+    send_gains.wait_recv()
+    for copy in sends_y:
+        copy.wait_recv()
+    squares = jnp.zeros((SPLIT, 128), F32)
+    for n in range(D // TILE):
+        pre = acc_out[n] + dot(yrx[...], wob[theirs, n * TILE : (n + 1) * TILE])
+        acc_out[n] = pre
+        squares = squares + pre[:, :128] * pre[:, :128] + pre[:, 128:] * pre[:, 128:]
+    mean = jnp.sum(squares, 1, keepdims=True) * F32(1.0 / D)
+    scale = lax.rsqrt(mean + F32(1e-05))
+
+    def normed(core, n):
+        gain = jnp.concatenate([gains[core, 2 * n : 2 * n + 1], gains[core, 2 * n + 1 : 2 * n + 2]], 1)
+        return (acc_out[core * (HALF // TILE) + n] * scale * gain).astype(BF)
+
+    sends_f = []
     for n in range(HALF // TILE):
-        mixed = acc_out[1, n] + term(c, n)
-        sends_o[n].wait_recv()
-        mixed = mixed + trx[n].astype(F32)
-        share[n] = mixed
-        squares = squares + mixed[:, :128] * mixed[:, :128] + mixed[:, 128:] * mixed[:, 128:]
-    sqtx[...] = squares
-    send_q = remote(sqtx, sqrx, q_s.at[0], q_r.at[0], me, other)
-    send_q.start()
-    send_q.wait_recv()
-    mean = jnp.sum(sqtx[...] + sqrx[...], 1, keepdims=True) * F32(1.0 / D)
-    scale = lax.rsqrt(mean + F32(1e-05))
+        cols = pl.ds(n * TILE, TILE)
+        otx[:, cols] = normed(other, n)
+        sends_f.append(remote(otx.at[:, cols], out.at[kept, cols], f_s.at[n], f_r.at[n], me, other))
+        sends_f[n].start()
     for n in range(HALF // TILE):
-        gains = jnp.concatenate([gnb[2 * n : 2 * n + 1], gnb[2 * n + 1 : 2 * n + 2]], 1).astype(F32)
-        out[:, n * TILE : (n + 1) * TILE] = (share[n] * scale * gains).astype(BF)
+        out[kept, n * TILE : (n + 1) * TILE] = normed(c, n)
+    for copy in sends_f:
+        copy.wait_recv()
 
     @pl.when(me < Z * PLANE - 1)
     def _():
@@ -337,9 +369,9 @@
             copy.wait_send()
 
     swap.wait_send()
-    for copy in sends1 + sends3 + sends_o + [send_q]:
+    for copy in sends1 + sends3 + sends_y + sends_f + [weights_out, send_gains]:
         copy.wait_send()
-    for chunk in range(2):
+    for chunk in range(len(CHUNKS)):
         for i in range(1, PLANE):
 
             @pl.when(line + i < PLANE)
@@ -356,17 +388,18 @@
         in_specs=[pl.BlockSpec(memory_space=pl.ANY)] * 9,
         out_specs=pl.BlockSpec(memory_space=pltpu.VMEM),
         scratch_shapes=[
-            vm((2, PADDED, HALF), BF), vm((D, 256), BF), vm((D, HALF), BF), vm((HALF, D), BF),
+            vm((2, PADDED, HALF), BF), vm((D, 256), BF), vm((D, HALF), BF), vm((D, D), BF),
             vm((3, 128), BF), vm((3, 128), BF), vm((3, HALF), BF), vm((8, 128), BF),
             vm((5, PADDED, TILE), F32), vm((PADDED, TILE), F32), vm((128, ROWS), F32), vm((128, ROWS), F32),
             vm((4, ROWS, TILE), BF), vm((HEADS, FEAT, ROWS), BF), vm((HEADS, ROWS, 256), BF),
             vm((HEADS, ROWS, TILE), F32),
             vm((8, FEAT, DV), BF), vm((Z, FEAT, DV), BF), vm((Z, FEAT, DV), F32), vm((FEAT, DV), BF),
             vm((PLANE, FEAT, DV), BF), vm((FEAT, DV), F32), vm((Z, FEAT, DV), BF), vm((Z, FEAT, DV), BF),
-            vm((2, 4, ROWS, TILE), F32), vm((4, ROWS, TILE), BF), vm((4, ROWS, TILE), BF), vm((4, ROWS, TILE), F32),
-            vm((ROWS, 128), F32), vm((ROWS, 128), F32),
-            dma((10,)), dma((1,)), dma((1,)), dma((2,)), dma((2,)), dma((2, 8)), dma((2, 8)),
-            dma((2, PLANE)), dma((2, PLANE)), dma((2, 8)), dma((2, 8)), dma((4,)), dma((4,)), dma((1,)), dma((1,)),
+            vm((8, SPLIT, TILE), F32), vm((ROWS, HALF), BF), vm((SPLIT, HALF), BF), vm((SPLIT, HALF), BF),
+            vm((2, 8, 128), F32),
+            dma((10,)), dma((1,)), dma((1,)), dma((2,)), dma((2,)), dma((4, 8)), dma((4, 8)),
+            dma((4, PLANE)), dma((4, PLANE)), dma((4, 8)), dma((4, 8)), dma((1,)), dma((1,)), dma((1,)), dma((1,)),
+            dma((8,)), dma((8,)), dma((4,)), dma((4,)), pltpu.SemaphoreType.REGULAR,
         ],
         compiler_params=pltpu.CompilerParams(
             collective_id=0, has_side_effects=True, vmem_limit_bytes=58 * 1024 * 1024

time: 48.1 us -> 45.6 us (0.948)
  Pallas kernels: 47 us -> 44.2 us
    pallas_call x1, Pallas kernels: 47 us -> 44.2 us  [body(): pl.pallas_call(kernel, out_shape=pltpu.VMEM((ROWS, HALF), BF), in_specs=[...]
where the time goes in v3:
time: 45.6 us; the launch traced here: 45.2 us
  Pallas kernels  44.2 us (97%)
  local copies, waits for them, and re-layouts  0.97 us (2%)
    pallas_call x1, Pallas kernels, body(): pl.pallas_call(kernel, out_shape=pltpu.VMEM((ROWS, HALF), BF), in_specs=[...  44.2 us
    unnamed x1, local copies, waits for them, and re-layouts  0.97 us

profile of v3, /device:TPU:5, one launch (start us, length us, event | category | flops | bytes accessed | tf_op | source)
XLA Modules:
  0.0 45.2 jit_solution(11328859942452512167)
XLA Ops:
  0.0 44.2 %shard_map.91 = bf16[512,1024]{1,0:T(8,128)(2,1)S(1)} custom-call(bf16[512,1024]{1,0:T(8,128)(2,1)} %tok.1, bf16[2048,128]{1,0:T(8,128)(2,1)} %wq.1, bf16[2048,128]{1,0:T(8,128)(2,1)} %wk.1, bf16[2048,1024]{1,0:T(8,128)(2,1)} %wv.1, bf16[3,128]{1,0:T(4,128)(2,1)} %cq.1, bf16[3,128]{1,0:T(4,128)(2,1)} %ck.1, bf16[3,1024]{1,0:T(4,128)(2,1)} %cv.1, ...), custom_call_target="tpu_custom_call" | custom-call | tf_op jit(solution)/shard_map/pallas_call | solution.py:385
  44.3 1.0 %copy.11 = bf16[512,1024]{1,0:T(8,128)(2,1)} copy(bf16[512,1024]{1,0:T(8,128)(2,1)S(1)} %shard_map.91) | data formatting | bytes 2097152

commit v4 on v3

--- a/solution.py
+++ b/solution.py
@@ -46,7 +46,7 @@
 def kernel(
     tok, wq, wk, wv, cq, ck, cv, wo, gn, out,
     xbuf, wqk, wvb, wob, cqb, ckb, cvb, gnb,
-    acc, pbuf, qt, kt, vbuf, pk, pq, num,
+    acc, pqk, pbuf, qt, kt, vbuf, pk, pq, num,
     loc, recv1, cbuf, ltx, lrx, offset, p3, recv3,
     acc_out, ybuf, yrx, otx, gains,
     lsem, tok_s, tok_r, halo_s, halo_r, s1_s, s1_r, l_s, l_r, s3_s, s3_r, w_s, w_r, g_s, g_r, o_s, o_r, f_s, f_r, ready,
@@ -140,7 +140,6 @@
         def _():
             rows[...] = jnp.zeros((HALO, HALF), BF)
 
-    halo_in(c)
     for copy in loads[:4]:
         copy.wait()
 
@@ -148,9 +147,10 @@
         return pl.ds(pl.multiple_of(pair * TILE, TILE), TILE)
 
     pairs = [lax.rem(lax.div(z, 2) + i, 4) for i in PAIR_ORDER]
-    acc[0] = dot(xbuf[c], wqk[mine, :])
+    acc[0] = dot(xbuf[c, HALO:PADDED], wqk[mine, :])
     for i, pair in enumerate(pairs):
-        acc[1 + i] = dot(xbuf[c], wvb[mine, columns(pair)])
+        acc[1 + i] = dot(xbuf[c, HALO:PADDED], wvb[mine, columns(pair)])
+    halo_in(c)
     halo_in(other)
     swap.wait_recv()
     weights_out = remote(wo, wob.at[mine], w_s.at[0], w_r.at[0], me, other)
@@ -161,18 +161,18 @@
     send_gains = remote(gains.at[c], gains.at[c], g_s.at[0], g_r.at[0], me, other)
     send_gains.start()
 
-    def convolved(taps):
-        return (
-            taps[0:1] * pbuf[16 : 16 + ROWS, :]
-            + taps[1:2] * pbuf[15 : 15 + ROWS, :]
-            + taps[2:3] * pbuf[14 : 14 + ROWS, :]
-        )
-
-    pbuf[...] = (acc[0] + dot(xbuf[other], wqk[theirs, :])).astype(BF).astype(F32)
-    taps = jnp.concatenate([cqb[...].astype(F32), ckb[...].astype(F32)], 1)
-    both = convolved(taps).T
-    qt[...] = both[0:128]
-    kt[...] = both[128:256]
+    def projected(i, own, rest):
+        more = dot(xbuf[other], rest)
+        first = more[0:HALO] + dot(xbuf[c, 0:HALO], own)
+        return jnp.concatenate([first, more[HALO:] + acc[i]], 0).astype(BF).astype(F32)
+
+    pqk[...] = projected(0, wqk[mine, :], wqk[theirs, :])
+    taps_k = ckb[...].astype(F32)
+    kt[...] = (
+        taps_k[0:1] * pqk[16 : 16 + ROWS, 128:256]
+        + taps_k[1:2] * pqk[15 : 15 + ROWS, 128:256]
+        + taps_k[2:3] * pqk[14 : 14 + ROWS, 128:256]
+    ).T
 
     def key_head(h, value):
         feats = features(kt[pl.ds(pl.multiple_of(h * FD, FD), FD), :]).astype(BF)
@@ -204,8 +204,13 @@
 
     routed = []
     for i, pair in enumerate(pairs):
-        pbuf[...] = (acc[1 + i] + dot(xbuf[other], wvb[theirs, columns(pair)])).astype(BF).astype(F32)
-        values = convolved(cvb[:, columns(pair)].astype(F32)).astype(BF)
+        pbuf[...] = projected(1 + i, wvb[mine, columns(pair)], wvb[theirs, columns(pair)])
+        taps = cvb[:, columns(pair)].astype(F32)
+        values = (
+            taps[0:1] * pbuf[16 : 16 + ROWS, :]
+            + taps[1:2] * pbuf[15 : 15 + ROWS, :]
+            + taps[2:3] * pbuf[14 : 14 + ROWS, :]
+        ).astype(BF)
         vbuf[pair] = values
         if PAIR_ORDER[i]:
             for b in range(2):
@@ -228,6 +233,12 @@
     half = lax.rem(z, 2)
     recv1[z] = key_head(z, jnp.where(half == 0, values[:, :DV], values[:, DV:]))
 
+    taps_q = cqb[...].astype(F32)
+    qt[...] = (
+        taps_q[0:1] * pqk[16 : 16 + ROWS, 0:128]
+        + taps_q[1:2] * pqk[15 : 15 + ROWS, 0:128]
+        + taps_q[2:3] * pqk[14 : 14 + ROWS, 0:128]
+    ).T
     ones = jnp.ones((ROWS, DV), BF)
 
     def query_head(h):
@@ -390,7 +401,7 @@
         scratch_shapes=[
             vm((2, PADDED, HALF), BF), vm((D, 256), BF), vm((D, HALF), BF), vm((D, D), BF),
             vm((3, 128), BF), vm((3, 128), BF), vm((3, HALF), BF), vm((8, 128), BF),
-            vm((5, PADDED, TILE), F32), vm((PADDED, TILE), F32), vm((128, ROWS), F32), vm((128, ROWS), F32),
+            vm((5, ROWS, TILE), F32), vm((PADDED, TILE), F32), vm((PADDED, TILE), F32), vm((128, ROWS), F32), vm((128, ROWS), F32),
             vm((4, ROWS, TILE), BF), vm((HEADS, FEAT, ROWS), BF), vm((HEADS, ROWS, 256), BF),
             vm((HEADS, ROWS, TILE), F32),
             vm((8, FEAT, DV), BF), vm((Z, FEAT, DV), BF), vm((Z, FEAT, DV), F32), vm((FEAT, DV), BF),

time: 45.6 us -> 45.8 us (level)
  no operation moved by 1% of the time
where the time goes in v4:
time: 45.8 us; the launch traced here: 45.4 us
  Pallas kernels  44.4 us (97%)
  local copies, waits for them, and re-layouts  0.97 us (2%)
    pallas_call x1, Pallas kernels, body(): pl.pallas_call(kernel, out_shape=pltpu.VMEM((ROWS, HALF), BF), in_specs=[...  44.4 us
    unnamed x1, local copies, waits for them, and re-layouts  0.97 us

profile of v4, /device:TPU:5, one launch (start us, length us, event | category | flops | bytes accessed | tf_op | source)
XLA Modules:
  0.0 45.4 jit_solution(6664748412642304313)
XLA Ops:
  0.0 44.4 %shard_map.91 = bf16[512,1024]{1,0:T(8,128)(2,1)S(1)} custom-call(bf16[512,1024]{1,0:T(8,128)(2,1)} %tok.1, bf16[2048,128]{1,0:T(8,128)(2,1)} %wq.1, bf16[2048,128]{1,0:T(8,128)(2,1)} %wk.1, bf16[2048,1024]{1,0:T(8,128)(2,1)} %wv.1, bf16[3,128]{1,0:T(4,128)(2,1)} %cq.1, bf16[3,128]{1,0:T(4,128)(2,1)} %ck.1, bf16[3,1024]{1,0:T(4,128)(2,1)} %cv.1, ...), custom_call_target="tpu_custom_call" | custom-call | tf_op jit(solution)/shard_map/pallas_call | solution.py:396
  44.4 1.0 %copy.11 = bf16[512,1024]{1,0:T(8,128)(2,1)} copy(bf16[512,1024]{1,0:T(8,128)(2,1)S(1)} %shard_map.91) | data formatting | bytes 2097152
